TPU v7x, 32 devices: a whole 2x2x4 slice. The times are simulated.
32 devices in a mesh: groups: 2 (over y), lat: 4 (over z), dm: 2 (over x), sub: 2 (over core).
Axes of the slice: x: 2, y: 2, z: 4, core: 2. Of those that a mesh axis runs over, the one named last changes fastest.
Arguments:
- tokens: bfloat16 [1024, 3584], P(('groups', 'lat'), 'dm'), parts along dimension 0, may hold values from -6 to 6
- cotangent: bfloat16 [1024, 3584], P(('groups', 'lat'), 'dm'), parts along dimension 0, may hold values from -6 to 6
- enc_weight: bfloat16 [3584, 8192], P('dm', ('lat', 'sub')), may hold values from -0.09375 to 0.09375
- enc_bias: float32 [8192], P(('lat', 'sub')), may hold values from -3 to 3
- threshold: float32 [8192], P(('lat', 'sub')), may hold values from 0.05 to 1.5
- dec_weight: bfloat16 [8192, 3584], P(('lat', 'sub'), 'dm'), may hold values from -0.0625 to 0.0625
- dec_bias: float32 [3584], P('dm'), may hold values from -3 to 3
- blocks: int32 [8, 8, 12], P('groups', ('lat', 'sub')), parts along dimension 0, may hold values from 0 to 127, as said below
- counts: int32 [8, 8], P('groups', ('lat', 'sub')), parts along dimension 0, may hold values from 0 to 12, as said below
Outputs:
- reconstruction: bfloat16 [1024, 3584], P(('groups', 'lat'), 'dm'), parts along dimension 0
- input_grad: bfloat16 [1024, 3584], P(('groups', 'lat'), 'dm'), parts along dimension 0
- attribution: float32 [16384], P(('groups', 'lat', 'sub')), parts along dimension 0
There are 2 independent parts, one for each index of `groups`. A program takes and returns all parts, laid end to end along the dimension named above; an argument that names none is the same for every part. Nothing has to cross between parts.
Inputs may be any that keep to these rules, and one draw needn't show every extreme that they name: blocks[t, h, k] is a block of shard h, h * 16 <= blocks[t, h, k] < (h + 1) * 16; the 12 slots of one tile and shard name different blocks. `counts`: in every draw some shard has all 12 slots live in every tile.
All inputs are finite; a program needn't handle non-finite values.
Results may differ from a plain program's by a relative error of at most 0.0049.
Values may be sent and summed in bfloat16 or wider, within the bound.
A program may use at most 128 MiB of HBM per device.

v0:
```python
import jax
import jax.numpy as jnp
from jax import lax
from jax.sharding import PartitionSpec as P

BLK = 64


band_width = 0.125


def local(tokens, cotangent, enc_weight, enc_bias, threshold, dec_weight, dec_bias, blocks, counts):
    whole_tokens, whole_grads = (
        lax.all_gather(tokens, "lat", axis=0, tiled=True),
        lax.all_gather(cotangent, "lat", axis=0, tiled=True),
    )
    tile_count = blocks.shape[0]
    slot_count = blocks.shape[2]
    width = tokens.shape[1]
    block_len = BLK
    block_count = enc_weight.shape[1] // block_len
    span = slot_count * block_len
    tile_len = whole_tokens.shape[0] // tile_count
    x_tiles = whole_tokens.reshape(tile_count, tile_len, width)
    g_tiles = whole_grads.reshape(tile_count, tile_len, width)
    flat_ids = (blocks[:, 0, :] % block_count).reshape(tile_count * slot_count)
    enc_sel = jnp.take(enc_weight.reshape(width, block_count, block_len), flat_ids, axis=1).reshape(
        width, tile_count, span
    )
    dec_sel = jnp.take(dec_weight.reshape(block_count, block_len, width), flat_ids, axis=0).reshape(
        tile_count, span, width
    )
    bias_sel = jnp.take(enc_bias.reshape(block_count, block_len), flat_ids, axis=0).reshape(
        tile_count, 1, span
    )
    level_sel = jnp.take(threshold.reshape(block_count, block_len), flat_ids, axis=0).reshape(
        tile_count, 1, span
    )
    live = (lax.broadcasted_iota(jnp.int32, (tile_count, slot_count), 1) < counts).astype(
        jnp.float32
    )
    gate_mask = jnp.repeat(live, block_len, axis=1)[:, None, :]
    enc_part = jnp.einsum("tnd,dtl->tnl", x_tiles, enc_sel, preferred_element_type=jnp.float32)
    dec_part = jnp.einsum("tnd,tld->tnl", g_tiles, dec_sel, preferred_element_type=jnp.float32)
    preact, grad_latent = lax.psum((enc_part, dec_part), "dm")
    preact = preact + bias_sel
    jump = gate_mask * jnp.clip((preact - level_sel) / band_width, 0.0, 1.0)
    active = preact * jump
    gated = grad_latent * jump
    scores = jnp.sum(active * grad_latent, axis=1)
    active_low = active.astype(jnp.bfloat16)
    gated_low = gated.astype(jnp.bfloat16)
    recon_rows = jnp.einsum(
        "tnl,tld->tnd", active_low, dec_sel, preferred_element_type=jnp.float32
    ).reshape(tile_count * tile_len, width)
    grad_rows = jnp.einsum(
        "tnl,dtl->tnd", gated_low, enc_sel, preferred_element_type=jnp.float32
    ).reshape(tile_count * tile_len, width)
    recon_part, grad_part = (
        lax.psum_scatter(recon_rows, "lat", scatter_dimension=0, tiled=True),
        lax.psum_scatter(grad_rows, "lat", scatter_dimension=0, tiled=True),
    )
    recon_full, grad_full = lax.psum((recon_part, grad_part), "sub")
    recon_out = (recon_full + dec_bias).astype(jnp.bfloat16)
    grad_out = grad_full.astype(jnp.bfloat16)
    picker = (
        flat_ids[:, None]
        == lax.broadcasted_iota(jnp.int32, (tile_count * slot_count, block_count), 1)
    ).astype(jnp.float32)
    slot_scores = scores.reshape(tile_count * slot_count, block_len)
    attribution = jnp.einsum(
        "sk,sb->kb",
        picker,
        slot_scores,
        precision=lax.Precision.HIGHEST,
        preferred_element_type=jnp.float32,
    ).reshape(block_count * block_len)
    return (recon_out, grad_out, attribution)


def solution(mesh):
    in_specs = (
        P(("groups", "lat"), "dm"),
        P(("groups", "lat"), "dm"),
        P("dm", ("lat", "sub")),
        P(("lat", "sub")),
        P(("lat", "sub")),
        P(("lat", "sub"), "dm"),
        P("dm"),
        P("groups", ("lat", "sub"), None),
        P("groups", ("lat", "sub")),
    )
    out_specs = (
        P(("groups", "lat"), "dm"),
        P(("groups", "lat"), "dm"),
        P(("groups", "lat", "sub")),
    )
    return jax.shard_map(local, mesh=mesh, in_specs=in_specs, out_specs=out_specs, check_vma=False)
```

profile of v0, /device:TPU:0, one launch (start us, length us, event | category | flops | bytes accessed | tf_op | source)
XLA Modules:
  0.0 366.6 jit_solution(18018007215399943549)
XLA Ops:
  7.2 0.7 all-gather.5.cloned.1.call-update
  7.9 0.7 all-gather.3.cloned.1.call-update
  8.7 0.7 compare_and_fusion.1
  9.5 0.1 broadcast_in_dim.38
  9.6 0.5 broadcast.145
  10.1 1.3 reduce.5
  11.4 0.1 squeeze.8
  11.5 5.9 %copy.15 = bf16[1792,1024]{0,1:T(8,128)(2,1)} copy(bf16[1792,1024]{1,0:T(8,128)(2,1)} %param.13) | data formatting | bytes 7340032 | tf_op args[2]
  17.5 9.2 %gather_fusion.1 = bf16[48,64,1792]{2,1,0:T(8,128)(2,1)} fusion(bf16[16,64,1792]{2,1,0:T(8,128)(2,1)} %bitcast.30, s32[1024]{0:T(1024)S(1)} %pad_clamp_fusion.1), kind=kCustom, calls=%fused_computation.3 | custom fusion | bytes 22020288 | tf_op jit(solution)/shard_map/jit(_take)/gather | solution.py:30
  26.7 9.1 %gather_fusion = bf16[48,1792,64]{1,2,0:T(8,128)(2,1)} fusion(bf16[1792,16,64]{0,2,1:T(8,128)(2,1)} %bitcast.26, s32[1024]{0:T(1024)S(1)} %pad_clamp_fusion.1), kind=kCustom, calls=%fused_computation.2 | custom fusion | bytes 22020288 | tf_op jit(solution)/shard_map/jit(_take)/gather | solution.py:27
  35.7 9.9 %bitcast_select_fusion = bf16[4,768,1792]{2,1,0:T(8,128)(2,1)} fusion(pred[4,768]{1,0:T(4,128)(4,1)S(1)} %broadcast_in_dim.38, bf16[4,768,1792]{2,1,0:T(8,128)(2,1)} %bitcast.29), kind=kLoop, calls=%fused_computation.4 | loop fusion | flops 5505024 | bytes 22023168 | tf_op jit(solution)/shard_map/jit(_take)/select_n | solution.py:30
  45.6 8.1 %all-gather.5.cloned.1.call-done = bf16[512,1792]{1,0:T(8,128)(2,1)} async-done(((bf16[128,1792]{1,0:T(8,128)(2,1)}), bf16[512,1792]{1,0:T(8,128)(2,1)}) %all-gather.5.cloned.1.call-update) | async-done | bytes 1835024 | tf_op jit(solution)/shard_map/all_gather | solution.py:15
  53.7 8.9 %convolution_bitcast_fusion = f32[4,128,768]{1,2,0:T(8,128)} fusion(bf16[4,768,1792]{2,1,0:T(8,128)(2,1)} %bitcast_select_fusion, bf16[4,128,1792]{2,1,0:T(8,128)(2,1)} %bitcast.36), kind=kOutput, calls=%fused_computation.14 | convolution fusion | flops 1409286144 | bytes 14417920 | tf_op jit(solution)/shard_map/tnd,tld->tnl/dot_general | solution.py:44
  62.6 33.0 %all-gather.3.cloned.1.call-done = bf16[512,1792]{1,0:T(8,128)(2,1)} async-done(((bf16[128,1792]{1,0:T(8,128)(2,1)}), bf16[512,1792]{1,0:T(8,128)(2,1)}) %all-gather.3.cloned.1.call-update) | async-done | bytes 1835024 | tf_op jit(solution)/shard_map/all_gather | solution.py:14
  95.6 7.3 %fusion.5 = f32[4,128,768]{1,2,0:T(8,128)} fusion(bf16[4,128,1792]{2,1,0:T(8,128)(2,1)} %bitcast.37, bf16[1792,4,768]{0,2,1:T(8,128)(2,1)} %bitcast.27, pred[4,768]{1,0:T(4,128)(4,1)S(1)} %broadcast_in_dim.38), kind=kOutput, calls=%fused_computation.15 | convolution fusion | flops 1414791168 | bytes 14420992 | tf_op jit(solution)/shard_map/tnd,dtl->tnl/dot_general | solution.py:43
  103.0 0.6 copy-done.2
  103.6 0.1 squeeze.9
  103.8 0.6 gather_fusion.2
  104.4 0.6 gather_fusion.3
  105.5 82.4 %all-reduce.7.cloned.1.call-done = (f32[4,128,768]{1,2,0:T(8,128)}, f32[4,128,768]{1,2,0:T(8,128)}) async-done(((f32[4,128,768]{1,2,0:T(8,128)}, f32[4,128,768]{1,2,0:T(8,128)}), (f32[4,128,768]{1,2,0:T(8,128)}, f32[4,128,768]{1,2,0:T(8,128)})) %all-reduce.7.cloned.1.call-update) | async-done | bytes 3145744 | tf_op jit(solution)/shard_map/psum | solution.py:45
  187.9 8.1 %fusion = f32[4,128,1792]{2,1,0:T(8,128)} fusion(bf16[1792,4,768]{0,2,1:T(8,128)(2,1)} %bitcast.28, pred[4,768]{1,0:T(4,128)(4,1)S(1)} %broadcast_in_dim.38, f32[4,128,768]{1,2,0:T(8,128)} %get-tuple-element.5, f32[4,128,768]{1,2,0:T(8,128)} %get-tuple-element.4, f32[4,768]{1,0:T(4,128)S(1)} %sub.10, f32[4,768]{1,0:T(4,128)S(1)} %mul.19, f32[4,768]{1,0:T(4,128)S(1)} %add.87), kind=kOutput, calls=%fused_computation.6 | convolution fusion | flops 1417543680 | bytes 17865728 | tf_op jit(solution)/shard_map/tnl,dtl->tnd/dot_general | solution.py:56
  196.1 1.3 copy-done
  197.4 6.8 %fusion.7 = f32[4,128,1792]{2,1,0:T(8,128)} fusion(bf16[4,768,1792]{2,1,0:T(8,128)(2,1)} %bitcast_select_fusion, f32[4,128,768]{1,2,0:T(8,128)S(1)} %copy-done, f32[4,768]{1,0:T(4,128)S(1)} %sub.10, f32[4,768]{1,0:T(4,128)S(1)} %mul.19, f32[4,768]{1,0:T(4,128)S(1)} %add.87), kind=kOutput, calls=%fused_computation.18 | convolution fusion | flops 1412038656 | bytes 16289792 | tf_op jit(solution)/shard_map/tnl,tld->tnd/dot_general | solution.py:53
  204.3 1.3 copy-done.1
  205.6 2.0 multiply_reduce_fusion
  207.7 0.3 fusion.21
  208.0 0.7 reshape.143
  208.7 55.9 %reduce-scatter.5.cloned.1.call-done = f32[128,1792]{1,0:T(8,128)} async-done(((f32[512,1792]{1,0:T(8,128)}), f32[128,1792]{1,0:T(8,128)}) %reduce-scatter.5.cloned.1.call-update) | async-done | bytes 917520 | tf_op jit(solution)/shard_map/reduce_scatter | solution.py:61
  264.6 71.1 %reduce-scatter.3.cloned.1.call-done = f32[128,1792]{1,0:T(8,128)} async-done(((f32[512,1792]{1,0:T(8,128)}), f32[128,1792]{1,0:T(8,128)}) %reduce-scatter.3.cloned.1.call-update) | async-done | bytes 917520 | tf_op jit(solution)/shard_map/reduce_scatter | solution.py:60
  335.7 7.1 %all-reduce.8 = bf16[128,1792]{1,0:T(8,128)(2,1)} all-reduce(f32[128,1792]{1,0:T(8,128)} %reduce-scatter.5.cloned.1.call-done), channel_id=1, replica_groups=mesh['groups'=2,'lat'=4,'dm'=2,'sub'=2] {'sub'}, use_global_device_ids=true, to_apply=%region_5.7 | all-reduce | flops 229376 | bytes 1376256 | tf_op jit(solution)/shard_map/psum | solution.py:63
  342.8 15.0 %all-reduce.5.cloned.1.call-done = f32[128,1792]{1,0:T(8,128)} async-done(((f32[128,1792]{1,0:T(8,128)}), f32[128,1792]{1,0:T(8,128)}) %all-reduce.5.cloned.1.call-update) | async-done | bytes 917520 | tf_op jit(solution)/shard_map/psum | solution.py:63
  357.8 2.0 add_convert_fusion
  (36 shorter events, 1.1 us)
Async XLA Ops:
  7.2 46.5 %all-gather.5.cloned.1.call-start = ((), (), s32[]{:S(2)}) async-start(), calls=%async_computation.5 | async-start | bytes 2293760 | tf_op jit(solution)/shard_map/all_gather | solution.py:15
  7.9 87.7 %all-gather.3.cloned.1.call-start = ((), (), s32[]{:S(2)}) async-start(), calls=%async_computation.2 | async-start | bytes 2293760 | tf_op jit(solution)/shard_map/all_gather | solution.py:14
  8.6 179.3 %all-reduce.7.cloned.1.call-start = ((), (), s32[]{:S(2)}) async-start(), calls=%async_computation.7 | async-start | bytes 6291456 | tf_op jit(solution)/shard_map/psum | solution.py:45
  102.9 0.7 copy-start.2
  102.9 0.8 copy-start.4
  102.9 0.8 copy-start.5
  102.9 2.4 copy-start.6
  102.9 161.7 %reduce-scatter.5.cloned.1.call-start = ((), (), s32[]{:S(2)}) async-start(), calls=%async_computation.6 | async-start | bytes 4587520 | tf_op jit(solution)/shard_map/reduce_scatter | solution.py:61
  196.0 1.4 copy-start
  196.0 139.6 %reduce-scatter.3.cloned.1.call-start = ((), (), s32[]{:S(2)}) async-start(), calls=%async_computation.3 | async-start | bytes 4587520 | tf_op jit(solution)/shard_map/reduce_scatter | solution.py:60
  204.2 1.4 copy-start.1
  204.2 153.5 %all-reduce.5.cloned.1.call-start = ((), (), s32[]{:S(2)}) async-start(), calls=%async_computation.4 | async-start | bytes 1835008 | tf_op jit(solution)/shard_map/psum | solution.py:63
  207.6 150.2 %copy-start.3 = (f32[1792]{0:T(1024)S(1)}, f32[1792]{0:T(1024)}, u32[]{:S(2)}) copy-start(f32[1792]{0:T(1024)} %param.17) | copy-start | bytes 21508
Sparse Core Ops, SparseCore 0:
  9.6 44.0 all-gather.4
  55.3 40.2 all-gather.2
  103.1 84.7 all-reduce.6
  196.1 68.4 reduce-scatter.4
  266.8 68.7 reduce-scatter.2
  338.0 19.7 all-reduce.4
where the time goes:
time: 367 us
  waiting for transfers between devices  267 us (73%)
  matrix products  31.4 us (9%)
  local copies, waits for them, and re-layouts  30.7 us (8%)
  other arithmetic  16.1 us (4%)
  between operations  14.2 us (4%)
  blocking collectives  7.13 us (2%)
    psum x1, waiting for transfers between devices, local(): preact, grad_latent = lax.psum((enc_part, dec_part), 'dm')  82.4 us
    reduce_scatter x1, waiting for transfers between devices, local(): lax.psum_scatter(recon_rows, 'lat', scatter_dimension=0, tiled=True)  71.1 us
    reduce_scatter x1, waiting for transfers between devices, local(): lax.psum_scatter(grad_rows, 'lat', scatter_dimension=0, tiled=True)  55.9 us
    all_gather x1, waiting for transfers between devices, local(): lax.all_gather(tokens, 'lat', axis=0, tiled=True)  33 us
    psum x1, waiting for transfers between devices, local(): recon_full, grad_full = lax.psum((recon_part, grad_part), 'sub')  15 us
    select_n x1, other arithmetic, local(): jnp.take(dec_weight.reshape(block_count, block_len, width), flat_ids, axi...  9.88 us
    unnamed x16, local copies, waits for them, and re-layouts  9.72 us
    gather x1, local copies, waits for them, and re-layouts, local(): jnp.take(dec_weight.reshape(block_count, block_len, width), flat_ids, axi...  9.19 us
  transfers between devices with their start and end apart: 6, of which 6 were waited for; matrix products, arithmetic and copies ran while one was open for 16% of the time, Pallas kernels for 0%

commit v1 on v0

--- a/solution.py
+++ b/solution.py
@@ -1,15 +1,294 @@
+import functools
+
 import jax
 import jax.numpy as jnp
 from jax import lax
+from jax.experimental import pallas as pl
+from jax.experimental.pallas import tpu as pltpu
 from jax.sharding import PartitionSpec as P
 
 BLK = 64
 
 
 band_width = 0.125
-
-
-def local(tokens, cotangent, enc_weight, enc_bias, threshold, dec_weight, dec_bias, blocks, counts):
+MESH = pl.DeviceIdType.MESH
+COL = 256
+
+
+def split3(v):
+    hi = v.astype(jnp.bfloat16)
+    rest = v - hi.astype(jnp.float32)
+    mid = rest.astype(jnp.bfloat16)
+    low = (rest - mid.astype(jnp.float32)).astype(jnp.bfloat16)
+    return hi, mid, low
+
+
+def rows_of(parts, width):
+    row = lax.broadcasted_iota(jnp.int32, (16, width), 0)
+    out = jnp.zeros((16, width), jnp.float32)
+    for i, part in enumerate(parts):
+        out = jnp.where(row == i, part.astype(jnp.float32), out)
+    return out.astype(jnp.bfloat16)
+
+
+def near_first(n, me, k):
+    out = 0
+    for z in range(n):
+        order = sorted(range(n), key=lambda t: (abs(t - z), t if z < n // 2 else -t))
+        out = jnp.where(me == z, order[k], out)
+    return out
+
+
+def dot(a, b):
+    return jnp.dot(a, b, preferred_element_type=jnp.float32)
+
+
+def dot_t(a, b):
+    return lax.dot_general(a, b, (((1,), (1,)), ((), ())), preferred_element_type=jnp.float32)
+
+
+def kernel(n, dims,
+           blocks_ref, counts_ref, tok_ref, cot_ref, enc_hbm, dec_hbm, bias_ref, level_ref, dbias_ref,
+           recon_ref, grad_ref, attr_ref,
+           enc, dec, xg, pick, stack, lat_stack, dense, xs_pre, xs_g, xr_pre, xr_g, side,
+           keep, sib_out, sib_in, term, home, own,
+           load_sem, z_send, z_recv, s_send, s_recv, xp_send, xp_recv, xq_send, xq_recv,
+           b_send, b_recv, h_send, h_recv, f_send, f_recv):
+    rows, width, latents, slots = dims
+    span = slots * BLK
+    z, x, c = lax.axis_index("lat"), lax.axis_index("dm"), lax.axis_index("sub")
+    tiles = [near_first(n, z, k) for k in range(n)]
+    other_c, other_x = 1 - c, 1 - x
+
+    loads = [
+        pltpu.make_async_copy(tok_ref, xg.at[0, z], load_sem.at[0]),
+        pltpu.make_async_copy(cot_ref, xg.at[1, z], load_sem.at[1]),
+        pltpu.make_async_copy(enc_hbm, enc, load_sem.at[2]),
+        pltpu.make_async_copy(dec_hbm, dec, load_sem.at[3]),
+    ]
+    for load in loads:
+        load.start()
+
+    barrier = pltpu.get_barrier_semaphore()
+    for k in range(1, n):
+        pl.semaphore_signal(barrier, inc=1, device_id={"lat": tiles[k]}, device_id_type=MESH)
+    pl.semaphore_signal(barrier, inc=1, device_id={"dm": other_x}, device_id_type=MESH)
+    pl.semaphore_signal(barrier, inc=1, device_id={"sub": other_c}, device_id_type=MESH)
+    pl.semaphore_wait(barrier, n + 1)
+
+    def copy(src, dst, send, recv, to):
+        return pltpu.make_async_remote_copy(
+            src_ref=src, dst_ref=dst, send_sem=send, recv_sem=recv, device_id=to, device_id_type=MESH)
+
+    ends = []
+
+    def send_if(cond, desc):
+        @pl.when(cond)
+        def _():
+            desc.start()
+
+        def finish():
+            @pl.when(cond)
+            def _():
+                desc.wait_send()
+        ends.append(finish)
+
+    def send(desc):
+        desc.start()
+        ends.append(desc.wait_send)
+
+    def up(t, k):
+        return copy(xg.at[c, t], xg.at[c, t], z_send.at[0, k], z_recv.at[t], {"lat": jnp.minimum(z + 1, n - 1)})
+
+    def down(t, k):
+        return copy(xg.at[c, t], xg.at[c, t], z_send.at[1, k], z_recv.at[t], {"lat": jnp.maximum(z - 1, 0)})
+
+    loads[0].wait()
+    loads[1].wait()
+    send_if(z < n - 1, up(z, 0))
+    send_if(z > 0, down(z, 0))
+
+    b3 = split3(bias_ref[...])
+    l3 = split3(level_ref[...])
+    stack[3 * rows:, :] = rows_of(b3 + l3, latents)
+    attr_ref[...] = jnp.zeros_like(attr_ref)
+    loads[2].wait()
+    loads[3].wait()
+
+    def ingest(k):
+        t = tiles[k]
+        up(t, k).wait_recv()
+        send_if((t < z) & (z < n - 1), up(t, k))
+        send_if((t > z) & (z > 0), down(t, k))
+        send(copy(xg.at[c, t], xg.at[c, t], s_send.at[k], s_recv.at[k], {"sub": other_c}))
+        copy(xg.at[other_c, t], xg.at[other_c, t], s_send.at[k], s_recv.at[k], {"sub": other_c}).wait_recv()
+
+    def partial(k):
+        t = tiles[k]
+
+        def first(i, carry):
+            cols = pl.ds(pl.multiple_of(i * COL, COL), COL)
+            p = dot(xg[0, t], enc[:, cols])
+            hi = p.astype(jnp.bfloat16)
+            stack[0:rows, cols] = hi
+            stack[rows:2 * rows, cols] = (p - hi.astype(jnp.float32)).astype(jnp.bfloat16)
+            stack[2 * rows:3 * rows, cols] = dot_t(xg[1, t], dec[cols, :]).astype(jnp.bfloat16)
+            return carry
+
+        lax.fori_loop(0, latents // COL, first, 0)
+
+        lane = lax.broadcasted_iota(jnp.int32, (1, span), 1)
+        slot = lane // BLK
+        target = jnp.full((1, span), -1, jnp.int32)
+        count = counts_ref[t, 0]
+        for s in range(slots):
+            base = jnp.where(s < count, (blocks_ref[t, s] % (latents // BLK)) * BLK, -2 * latents)
+            target = jnp.where(slot == s, base + lane % BLK, target)
+        for i in range(span // COL):
+            cols = slice(i * COL, (i + 1) * COL)
+            hit = lax.broadcasted_iota(jnp.int32, (latents, COL), 0) == target[:, cols]
+            one = jnp.where(hit, 1.0, 0.0).astype(jnp.bfloat16)
+            pick[k % 2, :, cols] = one
+            r = dot(stack[...], one)
+            xs_pre[k, :, cols] = r[0:rows] + r[rows:2 * rows]
+            xs_g[k, :, cols] = r[2 * rows:3 * rows].astype(jnp.bfloat16)
+            b = 3 * rows
+            side[k, 0:1, cols] = r[b:b + 1] + r[b + 1:b + 2] + r[b + 2:b + 3]
+            side[k, 1:2, cols] = r[b + 3:b + 4] + r[b + 4:b + 5] + r[b + 5:b + 6]
+        send(copy(xs_pre.at[k], xr_pre.at[k], xp_send.at[k], xp_recv.at[k], {"dm": other_x}))
+        send(copy(xs_g.at[k], xr_g.at[k], xq_send.at[k], xq_recv.at[k], {"dm": other_x}))
+
+    def second(k):
+        copy(xs_pre.at[k], xr_pre.at[k], xp_send.at[k], xp_recv.at[k], {"dm": other_x}).wait_recv()
+        copy(xs_g.at[k], xr_g.at[k], xq_send.at[k], xq_recv.at[k], {"dm": other_x}).wait_recv()
+        pre = xs_pre[k] + xr_pre[k] + side[k, 0:1, :]
+        gl = xs_g[k].astype(jnp.float32) + xr_g[k].astype(jnp.float32)
+        jump = jnp.clip((pre - side[k, 1:2, :]) / band_width, 0.0, 1.0)
+        active = pre * jump
+        lat_stack[0:rows, :] = active.astype(jnp.bfloat16)
+        lat_stack[rows:2 * rows, :] = (gl * jump).astype(jnp.bfloat16)
+        scores = jnp.sum(active * gl, axis=0, keepdims=True)
+        lat_stack[2 * rows:, :] = rows_of(split3(scores), span)
+
+        def spread(i, carry):
+            cols = pl.ds(pl.multiple_of(i * COL, COL), COL)
+            r = dot_t(lat_stack[...], pick[k % 2, cols, :])
+            dense[:, cols] = r[0:2 * rows].astype(jnp.bfloat16)
+            b = 2 * rows
+            attr_ref[0:1, cols] += r[b:b + 1] + r[b + 1:b + 2] + r[b + 2:b + 3]
+            return carry
+
+        lax.fori_loop(0, latents // COL, spread, 0)
+
+        def out(i, carry):
+            cols = pl.ds(pl.multiple_of(i * COL, COL), COL)
+            rec = dot(dense[0:rows, :], dec[:, cols])
+            gra = dot_t(dense[rows:2 * rows, :], enc[cols, :])
+            first_core = c == 0
+            keep[k, :, cols] = jnp.where(first_core, rec, gra)
+            sib_out[k, :, cols] = jnp.where(first_core, gra, rec).astype(jnp.bfloat16)
+            return carry
+
+        lax.fori_loop(0, width // COL, out, 0)
+        send(copy(sib_out.at[k], sib_in.at[k], b_send.at[k], b_recv.at[k], {"sub": other_c}))
+
+    def deliver(k):
+        copy(sib_out.at[k], sib_in.at[k], b_send.at[k], b_recv.at[k], {"sub": other_c}).wait_recv()
+        total = keep[k] + sib_in[k].astype(jnp.float32)
+        if k == 0:
+            own[...] = total
+        else:
+            term[k] = total.astype(jnp.bfloat16)
+            send(copy(term.at[k], home.at[z], h_send.at[k], h_recv.at[z], {"lat": tiles[k]}))
+
+    for k in range(n):
+        if k:
+            ingest(k)
+        partial(k)
+        if k >= 1:
+            second(k - 1)
+            deliver(k - 1)
+    second(n - 1)
+    deliver(n - 1)
+
+    total = own[...] + jnp.where(c == 0, dbias_ref[...], 0.0)
+    for k in range(1, n):
+        s = tiles[k]
+        copy(term.at[k], home.at[s], h_send.at[k], h_recv.at[s], {"lat": s}).wait_recv()
+        total += home[s].astype(jnp.float32)
+    final = total.astype(jnp.bfloat16)
+
+    give_recon = copy(recon_ref, recon_ref, f_send.at[0], f_recv.at[0], {"sub": other_c})
+    give_grad = copy(grad_ref, grad_ref, f_send.at[1], f_recv.at[1], {"sub": other_c})
+
+    @pl.when(c == 0)
+    def _():
+        recon_ref[...] = final
+        give_recon.start()
+        give_grad.wait_recv()
+        give_recon.wait_send()
+
+    @pl.when(c == 1)
+    def _():
+        grad_ref[...] = final
+        give_grad.start()
+        give_recon.wait_recv()
+        give_grad.wait_send()
+
+    for finish in ends:
+        finish()
+
+
+def fused(n, tokens, cotangent, enc_weight, enc_bias, threshold, dec_weight, dec_bias, blocks, counts):
+    rows, width = tokens.shape
+    latents = enc_weight.shape[1]
+    slots = blocks.shape[2]
+    span = slots * BLK
+    vmem, anywhere, smem = (pl.BlockSpec(memory_space=s) for s in (pltpu.VMEM, pl.ANY, pltpu.SMEM))
+    bf, f32 = jnp.bfloat16, jnp.float32
+    sem = pltpu.SemaphoreType.DMA
+    flops = 2 * 4 * n * rows * width * latents
+    recon, grad, attr = pl.pallas_call(
+        functools.partial(kernel, n, (rows, width, latents, slots)),
+        out_shape=(
+            jax.ShapeDtypeStruct((rows, width), bf),
+            jax.ShapeDtypeStruct((rows, width), bf),
+            jax.ShapeDtypeStruct((1, latents), f32),
+        ),
+        in_specs=[smem, smem, anywhere, anywhere, anywhere, anywhere, vmem, vmem, vmem],
+        out_specs=(vmem, vmem, vmem),
+        scratch_shapes=[
+            pltpu.VMEM((width, latents), bf),
+            pltpu.VMEM((latents, width), bf),
+            pltpu.VMEM((2, n, rows, width), bf),
+            pltpu.VMEM((2, latents, span), bf),
+            pltpu.VMEM((3 * rows + 16, latents), bf),
+            pltpu.VMEM((2 * rows + 16, span), bf),
+            pltpu.VMEM((2 * rows, latents), bf),
+            pltpu.VMEM((n, rows, span), f32),
+            pltpu.VMEM((n, rows, span), bf),
+            pltpu.VMEM((n, rows, span), f32),
+            pltpu.VMEM((n, rows, span), bf),
+            pltpu.VMEM((n, 8, span), f32),
+            pltpu.VMEM((n, rows, width), f32),
+            pltpu.VMEM((n, rows, width), bf),
+            pltpu.VMEM((n, rows, width), bf),
+            pltpu.VMEM((n, rows, width), bf),
+            pltpu.VMEM((n, rows, width), bf),
+            pltpu.VMEM((rows, width), f32),
+            sem((4,)), sem((2, n)), sem((n,)), sem((n,)), sem((n,)),
+            sem((n,)), sem((n,)), sem((n,)), sem((n,)),
+            sem((n,)), sem((n,)), sem((n,)), sem((n,)), sem((2,)), sem((2,)),
+        ],
+        compiler_params=pltpu.CompilerParams(
+            collective_id=0, has_side_effects=True, vmem_limit_bytes=56 * 1024 * 1024),
+        cost_estimate=pl.CostEstimate(flops=flops, bytes_accessed=4 * width * latents, transcendentals=0),
+    )(blocks[:, 0, :], counts, tokens, cotangent, enc_weight, dec_weight,
+      enc_bias[None, :], threshold[None, :], dec_bias[None, :])
+    return recon, grad, attr[0]
+
+
+def plain(tokens, cotangent, enc_weight, enc_bias, threshold, dec_weight, dec_bias, blocks, counts):
     whole_tokens, whole_grads = (
         lax.all_gather(tokens, "lat", axis=0, tiled=True),
         lax.all_gather(cotangent, "lat", axis=0, tiled=True),
@@ -79,6 +358,14 @@
 
 
 def solution(mesh):
+    n = mesh.shape["lat"]
+
+    def local(*args):
+        tokens, blocks = args[0], args[7]
+        if n == blocks.shape[0] and mesh.shape["dm"] == 2 and mesh.shape["sub"] == 2:
+            return fused(n, *args)
+        return plain(*args)
+
     in_specs = (
         P(("groups", "lat"), "dm"),
         P(("groups", "lat"), "dm"),

time: 367 us -> 113 us (0.31)
  waiting for transfers between devices: 267 us -> 0 us
  Pallas kernels: 0 us -> 105 us
  matrix products: 31.4 us -> 0 us
  local copies, waits for them, and re-layouts: 30.7 us -> 7.5 us
  other arithmetic: 16.1 us -> 0 us
  between operations: 14.2 us -> 0.64 us
  blocking collectives: 7.13 us -> 0 us
    reduce_scatter x2 -> x0, waiting for transfers between devices: 127 us -> none  [the longest x1 71.1 us: local(): lax.psum_scatter(recon_rows, 'lat', scatter_dimension=0, tiled=True)]
    pallas_call x0 -> x1, Pallas kernels: none -> 105 us  [fused(): pl.pallas_call(functools.partial(kernel, n, (rows, width, latents, slots)...]
    psum x2 -> x0, waiting for transfers between devices: 97.4 us -> none  [the longest x1 82.4 us: local(): preact, grad_latent = lax.psum((enc_part, dec_part), 'dm')]
    all_gather x2 -> x0, waiting for transfers between devices: 41.1 us -> none  [the longest x1 33 us: local(): lax.all_gather(tokens, 'lat', axis=0, tiled=True)]
    dot_general x5 -> x0, matrix products: 31.4 us -> none  [the longest x1 8.87 us: local(): jnp.einsum('tnd,tld->tnl', g_tiles, dec_sel, preferred_element_type=jnp.f...]
    gather x4 -> x0, local copies, waits for them, and re-layouts: 19.4 us -> none  [the longest x1 9.19 us: local(): jnp.take(dec_weight.reshape(block_count, block_len, width), flat_ids, axi...]
    select_n x4 -> x0, other arithmetic: 9.97 us -> none  [the longest x1 9.88 us: local(): jnp.take(dec_weight.reshape(block_count, block_len, width), flat_ids, axi...]
    psum x1 -> x0, blocking collectives: 7.13 us -> none  [local(): recon_full, grad_full = lax.psum((recon_part, grad_part), 'sub')]
  transfers between devices with their start and end apart: 6 -> 0, of which waited for: 6 -> 0; matrix products, arithmetic and copies ran while one was open for 16% -> 0% of each run, Pallas kernels for 0% -> 0%
where the time goes in v1:
time: 113 us
  Pallas kernels  105 us (93%)
  local copies, waits for them, and re-layouts  7.5 us (7%)
    pallas_call x1, Pallas kernels, fused(): pl.pallas_call(functools.partial(kernel, n, (rows, width, latents, slots)...  105 us
    unnamed x4, local copies, waits for them, and re-layouts  6.21 us

profile of v1, /device:TPU:0, one launch (start us, length us, event | category | flops | bytes accessed | tf_op | source)
XLA Modules:
  0.0 113.2 jit_solution(1730874952614355561)
XLA Ops:
  0.6 1.3 %copy.12.counts_ref = s32[4,1]{1,0:T(4,128)} copy(s32[4,1]{0,1:T(1,128)} %param.17) | data formatting | bytes 32 | tf_op args[8]
  1.9 1.3 %broadcast_in_dim.11.dbias_ref = f32[1,1792]{1,0:T(1,128)} reshape(f32[1792]{0:T(1024)} %param.15) | data formatting | bytes 14336 | tf_op jit(solution)/shard_map/broadcast_in_dim | solution.py:287
  3.2 105.0 %shard_map.112 = (bf16[128,1792]{1,0:T(8,128)(2,1)}, bf16[128,1792]{1,0:T(8,128)(2,1)}, f32[1,1024]{1,0:T(1,128)}) custom-call(s32[4,12]{1,0:T(4,128)} %bitcast.7, s32[4,1]{1,0:T(4,128)} %copy.12.counts_ref, bf16[128,1792]{1,0:T(8,128)(2,1)} %tok_ref.1, bf16[128,1792]{1,0:T(8,128)(2,1)} %cot_ref.1, bf16[1792,1024]{1,0:T(8,128)(2,1)} %enc_hbm.1, ...), custom_call_target="tpu_custom_call" | custom-call | flops 7516192768 | bytes 7340032 | tf_op jit(solution)/shard_map/pallas_call | solution.py:251
  108.3 1.8 %copy.16 = bf16[128,1792]{1,0:T(8,128)(2,1)} copy(bf16[128,1792]{1,0:T(8,128)(2,1)} %get-tuple-element.12) | data formatting | bytes 917504
  110.1 1.8 %copy.17 = bf16[128,1792]{1,0:T(8,128)(2,1)} copy(bf16[128,1792]{1,0:T(8,128)(2,1)} %get-tuple-element.13) | data formatting | bytes 917504
  111.9 1.3 %copy.18 = f32[1024]{0:T(1024)} copy(f32[1024]{0:T(1024)} %bitcast.4) | data formatting | bytes 8192

commit v2 on v1

--- a/solution.py
+++ b/solution.py
@@ -50,7 +50,7 @@
 def kernel(n, dims,
            blocks_ref, counts_ref, tok_ref, cot_ref, enc_hbm, dec_hbm, bias_ref, level_ref, dbias_ref,
            recon_ref, grad_ref, attr_ref,
-           enc, dec, xg, pick, stack, lat_stack, dense, xs_pre, xs_g, xr_pre, xr_g, side,
+           enc, dec, xg, back, stack, lat_stack, dense, xs, xr, scale_s, scale_r, side,
            keep, sib_out, sib_in, term, home, own,
            load_sem, z_send, z_recv, s_send, s_recv, xp_send, xp_recv, xq_send, xq_recv,
            b_send, b_recv, h_send, h_recv, f_send, f_recv):
@@ -110,18 +110,31 @@
 
     b3 = split3(bias_ref[...])
     l3 = split3(level_ref[...])
-    stack[3 * rows:, :] = rows_of(b3 + l3, latents)
+    stack[4 * rows:, :] = rows_of(b3 + l3, latents)
+    scale_s[...] = jnp.zeros_like(scale_s)
     attr_ref[...] = jnp.zeros_like(attr_ref)
     loads[2].wait()
     loads[3].wait()
 
-    def ingest(k):
+    def take_in(k):
         t = tiles[k]
         up(t, k).wait_recv()
         send_if((t < z) & (z < n - 1), up(t, k))
         send_if((t > z) & (z > 0), down(t, k))
         send(copy(xg.at[c, t], xg.at[c, t], s_send.at[k], s_recv.at[k], {"sub": other_c}))
+
+    def take_pair(k):
+        t = tiles[k]
         copy(xg.at[other_c, t], xg.at[other_c, t], s_send.at[k], s_recv.at[k], {"sub": other_c}).wait_recv()
+
+    def code(v):
+        top = jnp.max(jnp.abs(v), axis=0, keepdims=True)
+        grow = jnp.where(top > 1e-30, 32767.0 / jnp.maximum(top, 1e-30), 0.0)
+        return jnp.round(v * grow).astype(jnp.int32).astype(jnp.int16), top * (1.0 / 32767.0)
+
+    def swap(k, i):
+        return (copy(xs.at[k, i], xr.at[k, i], xp_send.at[k, i], xp_recv.at[k, i], {"dm": other_x}),
+                copy(scale_s.at[k, i], scale_r.at[k, i], xq_send.at[k, i], xq_recv.at[k, i], {"dm": other_x}))
 
     def partial(k):
         t = tiles[k]
@@ -132,7 +145,10 @@
             hi = p.astype(jnp.bfloat16)
             stack[0:rows, cols] = hi
             stack[rows:2 * rows, cols] = (p - hi.astype(jnp.float32)).astype(jnp.bfloat16)
-            stack[2 * rows:3 * rows, cols] = dot_t(xg[1, t], dec[cols, :]).astype(jnp.bfloat16)
+            q = dot_t(xg[1, t], dec[cols, :])
+            hi = q.astype(jnp.bfloat16)
+            stack[2 * rows:3 * rows, cols] = hi
+            stack[3 * rows:4 * rows, cols] = (q - hi.astype(jnp.float32)).astype(jnp.bfloat16)
             return carry
 
         lax.fori_loop(0, latents // COL, first, 0)
@@ -141,38 +157,65 @@
         slot = lane // BLK
         target = jnp.full((1, span), -1, jnp.int32)
         count = counts_ref[t, 0]
+        across = (lax.broadcasted_iota(jnp.int32, (BLK, latents), 1)
+                  - lax.broadcasted_iota(jnp.int32, (BLK, latents), 0))
         for s in range(slots):
             base = jnp.where(s < count, (blocks_ref[t, s] % (latents // BLK)) * BLK, -2 * latents)
             target = jnp.where(slot == s, base + lane % BLK, target)
+            back[k % 2, s * BLK:(s + 1) * BLK, :] = jnp.where(across == base, 1.0, 0.0).astype(jnp.bfloat16)
         for i in range(span // COL):
             cols = slice(i * COL, (i + 1) * COL)
             hit = lax.broadcasted_iota(jnp.int32, (latents, COL), 0) == target[:, cols]
             one = jnp.where(hit, 1.0, 0.0).astype(jnp.bfloat16)
-            pick[k % 2, :, cols] = one
             r = dot(stack[...], one)
-            xs_pre[k, :, cols] = r[0:rows] + r[rows:2 * rows]
-            xs_g[k, :, cols] = r[2 * rows:3 * rows].astype(jnp.bfloat16)
-            b = 3 * rows
-            side[k, 0:1, cols] = r[b:b + 1] + r[b + 1:b + 2] + r[b + 2:b + 3]
-            side[k, 1:2, cols] = r[b + 3:b + 4] + r[b + 4:b + 5] + r[b + 5:b + 6]
-        send(copy(xs_pre.at[k], xr_pre.at[k], xp_send.at[k], xp_recv.at[k], {"dm": other_x}))
-        send(copy(xs_g.at[k], xr_g.at[k], xq_send.at[k], xq_recv.at[k], {"dm": other_x}))
+            xs[k, i, 0], scale_s[k, i, 0:1, :] = code(r[0:rows] + r[rows:2 * rows])
+            xs[k, i, 1], scale_s[k, i, 1:2, :] = code(r[2 * rows:3 * rows] + r[3 * rows:4 * rows])
+            for desc in swap(k, i):
+                send(desc)
+            b = 4 * rows
+            side[k, i, 0:1, :] = r[b:b + 1] + r[b + 1:b + 2] + r[b + 2:b + 3]
+            side[k, i, 1:2, :] = r[b + 3:b + 4] + r[b + 4:b + 5] + r[b + 5:b + 6]
+
+    def whole(k, i, j):
+        return (xs[k, i, j].astype(jnp.int32).astype(jnp.float32) * scale_s[k, i, j:j + 1, :]
+                + xr[k, i, j].astype(jnp.int32).astype(jnp.float32) * scale_r[k, i, j:j + 1, :])
+
+    def rec(cols):
+        return dot(dense[0:rows, :], dec[:, cols])
+
+    def gra(cols):
+        return dot_t(dense[rows:2 * rows, :], enc[cols, :])
+
+    def for_columns(store, form):
+        def body(i, carry):
+            cols = pl.ds(pl.multiple_of(i * COL, COL), COL)
+            store(cols, form(cols))
+            return carry
+        lax.fori_loop(0, width // COL, body, 0)
+
+    def by_core(store, forms):
+        for core in range(2):
+            @pl.when(c == core)
+            def _():
+                for_columns(store, forms[core])
 
     def second(k):
-        copy(xs_pre.at[k], xr_pre.at[k], xp_send.at[k], xp_recv.at[k], {"dm": other_x}).wait_recv()
-        copy(xs_g.at[k], xr_g.at[k], xq_send.at[k], xq_recv.at[k], {"dm": other_x}).wait_recv()
-        pre = xs_pre[k] + xr_pre[k] + side[k, 0:1, :]
-        gl = xs_g[k].astype(jnp.float32) + xr_g[k].astype(jnp.float32)
-        jump = jnp.clip((pre - side[k, 1:2, :]) / band_width, 0.0, 1.0)
-        active = pre * jump
-        lat_stack[0:rows, :] = active.astype(jnp.bfloat16)
-        lat_stack[rows:2 * rows, :] = (gl * jump).astype(jnp.bfloat16)
-        scores = jnp.sum(active * gl, axis=0, keepdims=True)
-        lat_stack[2 * rows:, :] = rows_of(split3(scores), span)
+        for i in range(span // COL):
+            cols = slice(i * COL, (i + 1) * COL)
+            for desc in swap(k, i):
+                desc.wait_recv()
+            pre = whole(k, i, 0) + side[k, i, 0:1, :]
+            gl = whole(k, i, 1)
+            jump = jnp.clip((pre - side[k, i, 1:2, :]) / band_width, 0.0, 1.0)
+            active = pre * jump
+            lat_stack[0:rows, cols] = active.astype(jnp.bfloat16)
+            lat_stack[rows:2 * rows, cols] = (gl * jump).astype(jnp.bfloat16)
+            scores = jnp.sum(active * gl, axis=0, keepdims=True)
+            lat_stack[2 * rows:, cols] = rows_of(split3(scores), COL)
 
         def spread(i, carry):
             cols = pl.ds(pl.multiple_of(i * COL, COL), COL)
-            r = dot_t(lat_stack[...], pick[k % 2, cols, :])
+            r = dot(lat_stack[...], back[k % 2, :, cols])
             dense[:, cols] = r[0:2 * rows].astype(jnp.bfloat16)
             b = 2 * rows
             attr_ref[0:1, cols] += r[b:b + 1] + r[b + 1:b + 2] + r[b + 2:b + 3]
@@ -180,21 +223,19 @@
 
         lax.fori_loop(0, latents // COL, spread, 0)
 
-        def out(i, carry):
-            cols = pl.ds(pl.multiple_of(i * COL, COL), COL)
-            rec = dot(dense[0:rows, :], dec[:, cols])
-            gra = dot_t(dense[rows:2 * rows, :], enc[cols, :])
-            first_core = c == 0
-            keep[k, :, cols] = jnp.where(first_core, rec, gra)
-            sib_out[k, :, cols] = jnp.where(first_core, gra, rec).astype(jnp.bfloat16)
-            return carry
-
-        lax.fori_loop(0, width // COL, out, 0)
+        def store(cols, v):
+            sib_out[k, :, cols] = v.astype(jnp.bfloat16)
+
+        by_core(store, (gra, rec))
         send(copy(sib_out.at[k], sib_in.at[k], b_send.at[k], b_recv.at[k], {"sub": other_c}))
 
     def deliver(k):
+        def store(cols, v):
+            keep[:, cols] = v
+
+        by_core(store, (rec, gra))
         copy(sib_out.at[k], sib_in.at[k], b_send.at[k], b_recv.at[k], {"sub": other_c}).wait_recv()
-        total = keep[k] + sib_in[k].astype(jnp.float32)
+        total = keep[...] + sib_in[k].astype(jnp.float32)
         if k == 0:
             own[...] = total
         else:
@@ -203,10 +244,13 @@
 
     for k in range(n):
         if k:
-            ingest(k)
+            take_pair(k)
         partial(k)
-        if k >= 1:
+        if k:
             second(k - 1)
+        if k + 1 < n:
+            take_in(k + 1)
+        if k:
             deliver(k - 1)
     second(n - 1)
     deliver(n - 1)
@@ -244,6 +288,7 @@
     latents = enc_weight.shape[1]
     slots = blocks.shape[2]
     span = slots * BLK
+    parts = span // COL
     vmem, anywhere, smem = (pl.BlockSpec(memory_space=s) for s in (pltpu.VMEM, pl.ANY, pltpu.SMEM))
     bf, f32 = jnp.bfloat16, jnp.float32
     sem = pltpu.SemaphoreType.DMA
@@ -261,23 +306,23 @@
             pltpu.VMEM((width, latents), bf),
             pltpu.VMEM((latents, width), bf),
             pltpu.VMEM((2, n, rows, width), bf),
-            pltpu.VMEM((2, latents, span), bf),
-            pltpu.VMEM((3 * rows + 16, latents), bf),
+            pltpu.VMEM((2, span, latents), bf),
+            pltpu.VMEM((4 * rows + 16, latents), bf),
             pltpu.VMEM((2 * rows + 16, span), bf),
             pltpu.VMEM((2 * rows, latents), bf),
-            pltpu.VMEM((n, rows, span), f32),
-            pltpu.VMEM((n, rows, span), bf),
-            pltpu.VMEM((n, rows, span), f32),
-            pltpu.VMEM((n, rows, span), bf),
-            pltpu.VMEM((n, 8, span), f32),
-            pltpu.VMEM((n, rows, width), f32),
+            pltpu.VMEM((n, parts, 2, rows, COL), jnp.int16),
+            pltpu.VMEM((n, parts, 2, rows, COL), jnp.int16),
+            pltpu.VMEM((n, parts, 8, COL), f32),
+            pltpu.VMEM((n, parts, 8, COL), f32),
+            pltpu.VMEM((n, parts, 8, COL), f32),
+            pltpu.VMEM((rows, width), f32),
             pltpu.VMEM((n, rows, width), bf),
             pltpu.VMEM((n, rows, width), bf),
             pltpu.VMEM((n, rows, width), bf),
             pltpu.VMEM((n, rows, width), bf),
             pltpu.VMEM((rows, width), f32),
             sem((4,)), sem((2, n)), sem((n,)), sem((n,)), sem((n,)),
-            sem((n,)), sem((n,)), sem((n,)), sem((n,)),
+            sem((n, parts)), sem((n, parts)), sem((n, parts)), sem((n, parts)),
             sem((n,)), sem((n,)), sem((n,)), sem((n,)), sem((2,)), sem((2,)),
         ],
         compiler_params=pltpu.CompilerParams(

time: 113 us -> 102 us (0.903)
  Pallas kernels: 105 us -> 93.9 us
    pallas_call x1, Pallas kernels: 105 us -> 93.9 us  [fused(): pl.pallas_call(functools.partial(kernel, n, (rows, width, latents, slots)...]
where the time goes in v2:
time: 102 us
  Pallas kernels  93.9 us (92%)
  local copies, waits for them, and re-layouts  7.5 us (7%)
    pallas_call x1, Pallas kernels, fused(): pl.pallas_call(functools.partial(kernel, n, (rows, width, latents, slots)...  93.9 us
    unnamed x4, local copies, waits for them, and re-layouts  6.21 us

profile of v2, /device:TPU:0, one launch (start us, length us, event | category | flops | bytes accessed | tf_op | source)
XLA Modules:
  0.0 102.1 jit_solution(14546105207647294113)
XLA Ops:
  0.6 1.3 %copy.12.counts_ref = s32[4,1]{1,0:T(4,128)} copy(s32[4,1]{0,1:T(1,128)} %param.17) | data formatting | bytes 32 | tf_op args[8]
  1.9 1.3 %broadcast_in_dim.11.dbias_ref = f32[1,1792]{1,0:T(1,128)} reshape(f32[1792]{0:T(1024)} %param.15) | data formatting | bytes 14336 | tf_op jit(solution)/shard_map/broadcast_in_dim | solution.py:332
  3.2 93.9 %shard_map.112 = (bf16[128,1792]{1,0:T(8,128)(2,1)}, bf16[128,1792]{1,0:T(8,128)(2,1)}, f32[1,1024]{1,0:T(1,128)}) custom-call(s32[4,12]{1,0:T(4,128)} %bitcast.7, s32[4,1]{1,0:T(4,128)} %copy.12.counts_ref, bf16[128,1792]{1,0:T(8,128)(2,1)} %tok_ref.1, bf16[128,1792]{1,0:T(8,128)(2,1)} %cot_ref.1, bf16[1792,1024]{1,0:T(8,128)(2,1)} %enc_hbm.1, ...), custom_call_target="tpu_custom_call" | custom-call | flops 7516192768 | bytes 7340032 | tf_op jit(solution)/shard_map/pallas_call | solution.py:296
  97.2 1.8 %copy.16 = bf16[128,1792]{1,0:T(8,128)(2,1)} copy(bf16[128,1792]{1,0:T(8,128)(2,1)} %get-tuple-element.12) | data formatting | bytes 917504
  99.0 1.8 %copy.17 = bf16[128,1792]{1,0:T(8,128)(2,1)} copy(bf16[128,1792]{1,0:T(8,128)(2,1)} %get-tuple-element.13) | data formatting | bytes 917504
  100.8 1.3 %copy.18 = f32[1024]{0:T(1024)} copy(f32[1024]{0:T(1024)} %bitcast.4) | data formatting | bytes 8192

commit v3 on v2

--- a/solution.py
+++ b/solution.py
@@ -229,6 +229,30 @@
         by_core(store, (gra, rec))
         send(copy(sib_out.at[k], sib_in.at[k], b_send.at[k], b_recv.at[k], {"sub": other_c}))
 
+    def fed(k):
+        t = tiles[k]
+        return ((t > z) & (z > 0)) | ((t < z) & (z < n - 1))
+
+    def landing(slot, j):
+        return home.at[slot, j]
+
+    def onward(k, j):
+        t = tiles[k]
+        step = jnp.where(t > z, z + 1, z - 1)
+        slot = jnp.where(t == z + 1, n, t)
+        return copy(term.at[k, j], landing(slot, j), h_send.at[k, j], h_recv.at[slot, j], {"lat": step})
+
+    def arrived(slot, j):
+        to = jnp.where(z > 0, z - 1, z + 1)
+        copy(term.at[1, j], landing(slot, j), h_send.at[1, j], h_recv.at[slot, j], {"lat": to}).wait_recv()
+        return home[slot, j].astype(jnp.float32)
+
+    def relay(k, j):
+        @pl.when(fed(k))
+        def _():
+            term[k, j] = (term[k, j].astype(jnp.float32) + arrived(tiles[k], j)).astype(jnp.bfloat16)
+            onward(k, j).start()
+
     def deliver(k):
         def store(cols, v):
             keep[:, cols] = v
@@ -239,8 +263,14 @@
         if k == 0:
             own[...] = total
         else:
-            term[k] = total.astype(jnp.bfloat16)
-            send(copy(term.at[k], home.at[z], h_send.at[k], h_recv.at[z], {"lat": tiles[k]}))
+            for j in range(width // COL):
+                term[k, j] = total[:, j * COL:(j + 1) * COL].astype(jnp.bfloat16)
+
+
+            @pl.when(jnp.logical_not(fed(k)))
+            def _():
+                for j in range(width // COL):
+                    onward(k, j).start()
 
     for k in range(n):
         if k:
@@ -253,13 +283,19 @@
         if k:
             deliver(k - 1)
     second(n - 1)
+    for j in range(width // COL):
+        relay(2, j)
     deliver(n - 1)
-
+    for j in range(width // COL):
+        relay(3, j)
+        relay(1, j)
+
+    for there, slot in ((z > 0, n), (z < n - 1, z)):
+        @pl.when(there)
+        def _():
+            for j in range(width // COL):
+                own[:, j * COL:(j + 1) * COL] += arrived(slot, j)
     total = own[...] + jnp.where(c == 0, dbias_ref[...], 0.0)
-    for k in range(1, n):
-        s = tiles[k]
-        copy(term.at[k], home.at[s], h_send.at[k], h_recv.at[s], {"lat": s}).wait_recv()
-        total += home[s].astype(jnp.float32)
     final = total.astype(jnp.bfloat16)
 
     give_recon = copy(recon_ref, recon_ref, f_send.at[0], f_recv.at[0], {"sub": other_c})
@@ -279,6 +315,9 @@
         give_recon.wait_recv()
         give_grad.wait_send()
 
+    for k in range(1, n):
+        for j in range(width // COL):
+            onward(k, j).wait_send()
     for finish in ends:
         finish()
 
@@ -318,12 +357,12 @@
             pltpu.VMEM((rows, width), f32),
             pltpu.VMEM((n, rows, width), bf),
             pltpu.VMEM((n, rows, width), bf),
-            pltpu.VMEM((n, rows, width), bf),
-            pltpu.VMEM((n, rows, width), bf),
+            pltpu.VMEM((n, width // COL, rows, COL), bf),
+            pltpu.VMEM((n + 1, width // COL, rows, COL), bf),
             pltpu.VMEM((rows, width), f32),
             sem((4,)), sem((2, n)), sem((n,)), sem((n,)), sem((n,)),
             sem((n, parts)), sem((n, parts)), sem((n, parts)), sem((n, parts)),
-            sem((n,)), sem((n,)), sem((n,)), sem((n,)), sem((2,)), sem((2,)),
+            sem((n,)), sem((n,)), sem((n, width // COL)), sem((n + 1, width // COL)), sem((2,)), sem((2,)),
         ],
         compiler_params=pltpu.CompilerParams(
             collective_id=0, has_side_effects=True, vmem_limit_bytes=56 * 1024 * 1024),
@@ -407,7 +446,7 @@
 
     def local(*args):
         tokens, blocks = args[0], args[7]
-        if n == blocks.shape[0] and mesh.shape["dm"] == 2 and mesh.shape["sub"] == 2:
+        if n == 4 and n == blocks.shape[0] and mesh.shape["dm"] == 2 and mesh.shape["sub"] == 2:
             return fused(n, *args)
         return plain(*args)
 

time: 102 us -> 113 us (1.11)
  Pallas kernels: 93.9 us -> 104 us
    pallas_call x1, Pallas kernels: 93.9 us -> 104 us  [fused(): pl.pallas_call(functools.partial(kernel, n, (rows, width, latents, slots)...]
where the time goes in v3:
time: 113 us
  Pallas kernels  104 us (92%)
  local copies, waits for them, and re-layouts  7.5 us (7%)
    pallas_call x1, Pallas kernels, fused(): pl.pallas_call(functools.partial(kernel, n, (rows, width, latents, slots)...  104 us
    unnamed x4, local copies, waits for them, and re-layouts  6.21 us

profile of v3, /device:TPU:0, one launch (start us, length us, event | category | flops | bytes accessed | tf_op | source)
XLA Modules:
  0.0 112.5 jit_solution(17229064457558711678)
XLA Ops:
  0.6 1.3 %copy.12.counts_ref = s32[4,1]{1,0:T(4,128)} copy(s32[4,1]{0,1:T(1,128)} %param.17) | data formatting | bytes 32 | tf_op args[8]
  1.9 1.3 %broadcast_in_dim.11.dbias_ref = f32[1,1792]{1,0:T(1,128)} reshape(f32[1792]{0:T(1024)} %param.15) | data formatting | bytes 14336 | tf_op jit(solution)/shard_map/broadcast_in_dim | solution.py:371
  3.2 104.4 %shard_map.112 = (bf16[128,1792]{1,0:T(8,128)(2,1)}, bf16[128,1792]{1,0:T(8,128)(2,1)}, f32[1,1024]{1,0:T(1,128)}) custom-call(s32[4,12]{1,0:T(4,128)} %bitcast.7, s32[4,1]{1,0:T(4,128)} %copy.12.counts_ref, bf16[128,1792]{1,0:T(8,128)(2,1)} %tok_ref.1, bf16[128,1792]{1,0:T(8,128)(2,1)} %cot_ref.1, bf16[1792,1024]{1,0:T(8,128)(2,1)} %enc_hbm.1, ...), custom_call_target="tpu_custom_call" | custom-call | flops 7516192768 | bytes 7340032 | tf_op jit(solution)/shard_map/pallas_call | solution.py:335
  107.6 1.8 %copy.16 = bf16[128,1792]{1,0:T(8,128)(2,1)} copy(bf16[128,1792]{1,0:T(8,128)(2,1)} %get-tuple-element.12) | data formatting | bytes 917504
  109.5 1.8 %copy.17 = bf16[128,1792]{1,0:T(8,128)(2,1)} copy(bf16[128,1792]{1,0:T(8,128)(2,1)} %get-tuple-element.13) | data formatting | bytes 917504
  111.3 1.3 %copy.18 = f32[1024]{0:T(1024)} copy(f32[1024]{0:T(1024)} %bitcast.4) | data formatting | bytes 8192
